TPU v7x, 32 devices: a whole 2x2x4 slice. The times are simulated.
32 devices in a mesh: groups: 2 (over y), mp: 4 (over z), heads: 4 (over x, core).
Axes of the slice: x: 2, y: 2, z: 4, core: 2. Of those that a mesh axis runs over, the one named last changes fastest.
Arguments:
- stream: bfloat16 [16, 8192], P('groups', ('mp', 'heads')), parts along dimension 0, may hold values from -6 to 6
- in_gain: float32 [8192], P('mp'), may hold values from 0.5 to 1.5
- w_inner: bfloat16 [8192, 2, 128, 64], P('mp', None, 'heads'), may hold values from -0.09375 to 0.09375
- w_state: bfloat16 [8192, 2, 4, 256], P('mp'), may hold values from -0.0625 to 0.0625
- w_step: bfloat16 [8192, 128], P('mp', 'heads'), may hold values from -0.0625 to 0.0625
- step_bias: float32 [128], P('heads'), may hold values from -3 to 1
- decay_scale: float32 [128], P('heads'), may hold values from 0.02 to 8
- skip_gain: float32 [128], P('heads'), may hold values from 0.5 to 1.5
- conv_inner: float32 [4, 128, 64], P(None, 'heads', 'mp'), may hold values from -3 to 3
- conv_state_weight: float32 [4, 2, 4, 256], replicated, may hold values from -3 to 3
- history_inner: bfloat16 [16, 3, 128, 64], P('groups', None, 'heads', 'mp'), parts along dimension 0, may hold values from -6 to 6
- history_state: bfloat16 [16, 3, 2, 4, 256], P('groups'), parts along dimension 0, may hold values from -6 to 6
- ssm_state: float32 [16, 128, 64, 256], P('groups', 'heads', 'mp'), parts along dimension 0, may hold values from -4 to 4
- norm_gain: float32 [128, 64], P('heads', 'mp'), may hold values from 0.5 to 1.5
- w_out: bfloat16 [128, 64, 8192], P('heads', None, 'mp'), may hold values from -0.09375 to 0.09375
Outputs:
- residual_out: bfloat16 [8, 16, 8192], P(None, 'groups', ('mp', 'heads')), parts along dimension 1
- state_out: float32 [16, 128, 64, 256], P('groups', 'heads', 'mp'), parts along dimension 0
- inner_hist_out: bfloat16 [16, 3, 128, 64], P('groups', None, 'heads', 'mp'), parts along dimension 0
- state_hist_out: bfloat16 [16, 3, 2, 4, 256], P('groups'), parts along dimension 0
There are 2 independent parts, one for each index of `groups`. A program takes and returns all parts, laid end to end along the dimension named above; an argument that names none is the same for every part. Nothing has to cross between parts.
All inputs are finite; a program needn't handle non-finite values.
Results may differ from a plain program's by a relative error of at most 0.018.
Values may be sent and summed in bfloat16 or wider, within the bound.
A program may use at most 192 MiB of HBM per device.

v0:
```python
import jax
import jax.numpy as jnp
from jax import lax
from jax.sharding import PartitionSpec as P

D = 8192
NH = 128
NG = 4
STEPS = 8


EPSILON = 1e-05


def causal_conv(history, incoming, kernel):
    window = jnp.concatenate([history, incoming[:, None]], axis=1)
    weighted = jnp.sum(window.astype(jnp.float32) * kernel[None], axis=1)
    return (jax.nn.silu(weighted), window[:, 1:])


def body(
    stream,
    in_gain,
    w_inner,
    w_state,
    w_step,
    step_bias,
    decay_scale,
    skip_gain,
    conv_inner,
    conv_state_weight,
    history_inner,
    history_state,
    ssm_state,
    norm_gain,
    w_out,
):
    row_count = stream.shape[0]
    local_width = w_inner.shape[0]
    local_heads = w_inner.shape[2]
    head_size = w_inner.shape[3]
    part_size = ssm_state.shape[2]
    group_count = w_state.shape[2]
    state_size = w_state.shape[3]
    flat_inner = w_inner.reshape(local_width, 2 * local_heads * head_size)
    flat_state = w_state.reshape(local_width, 2 * group_count * state_size)
    per_group = NH // NG
    head_ids = lax.axis_index("heads") * local_heads + jnp.arange(local_heads, dtype=jnp.int32)
    member = (head_ids // per_group)[:, None] == jnp.arange(group_count, dtype=jnp.int32)[None, :]
    current = stream
    hist_inner = history_inner
    hist_state = history_state
    hidden = ssm_state
    written = []
    for step_index in range(STEPS):
        values = lax.all_gather(current, "heads", axis=1, tiled=True).astype(jnp.float32)
        scaled = (values * in_gain[None, :]).astype(jnp.bfloat16)
        part_inner = jnp.dot(scaled, flat_inner, preferred_element_type=jnp.float32)
        part_state = jnp.dot(scaled, flat_state, preferred_element_type=jnp.float32)
        part_step = jnp.dot(scaled, w_step, preferred_element_type=jnp.float32)
        part_sq = jnp.sum(values * values, axis=1)
        summed_all, sum_state, sum_step, sum_sq = lax.psum(
            (part_inner, part_state, part_step, part_sq), "mp"
        )
        proj_inner = lax.dynamic_slice_in_dim(
            summed_all.reshape(row_count, 2, local_heads, head_size),
            lax.axis_index("mp") * part_size,
            part_size,
            3,
        )
        inv_rms = lax.rsqrt(sum_sq / D + EPSILON)[:, None]
        proj_inner = proj_inner * inv_rms[:, :, None, None]
        conv_x, hist_inner = causal_conv(
            hist_inner, proj_inner[:, 0].astype(jnp.bfloat16), conv_inner
        )
        incoming_bc = (
            (sum_state * inv_rms)
            .reshape(row_count, 2, group_count, state_size)
            .astype(jnp.bfloat16)
        )
        conv_bc, hist_state = causal_conv(hist_state, incoming_bc, conv_state_weight)
        head_b = jnp.sum(jnp.where(member[None, :, :, None], conv_bc[:, 0][:, None], 0.0), axis=2)
        head_c = jnp.sum(jnp.where(member[None, :, :, None], conv_bc[:, 1][:, None], 0.0), axis=2)
        step_dt = jax.nn.softplus(sum_step * inv_rms + step_bias[None, :])
        decay_rate = jnp.exp(-step_dt * decay_scale[None, :])
        hidden = (
            decay_rate[:, :, None, None] * hidden
            + (step_dt[:, :, None] * conv_x)[:, :, :, None] * head_b[:, :, None, :]
        )
        reading = (
            jnp.sum(hidden * head_c[:, :, None, :], axis=3) + skip_gain[None, :, None] * conv_x
        )
        gated_out = reading * jax.nn.silu(proj_inner[:, 1])
        head_sq = jnp.sum(gated_out * gated_out, axis=2)
        group_part = jnp.sum(jnp.where(member[None], head_sq[:, :, None], 0.0), axis=1)
        group_total = lax.psum(group_part, ("mp", "heads"))
        head_total = jnp.sum(jnp.where(member[None], group_total[:, None, :], 0.0), axis=2)
        mean_sq = head_total / (per_group * head_size)
        normed = (gated_out * lax.rsqrt(mean_sq + EPSILON)[:, :, None] * norm_gain[None]).astype(
            jnp.bfloat16
        )
        partial_out = jnp.einsum(
            "rhp,hpd->rd",
            lax.all_gather(normed, "mp", axis=2, tiled=True),
            w_out,
            preferred_element_type=jnp.float32,
        )
        update = lax.psum_scatter(partial_out, "heads", scatter_dimension=1, tiled=True)
        current = (current.astype(jnp.float32) + update).astype(jnp.bfloat16)
        written.append(current)
    return (jnp.stack(written), hidden, hist_inner, hist_state)


def solution(mesh):
    return jax.shard_map(
        body,
        mesh=mesh,
        in_specs=(
            P("groups", ("mp", "heads")),
            P("mp"),
            P("mp", None, "heads", None),
            P("mp", None, None, None),
            P("mp", "heads"),
            P("heads"),
            P("heads"),
            P("heads"),
            P(None, "heads", "mp"),
            P(),
            P("groups", None, "heads", "mp"),
            P("groups", None, None, None, None),
            P("groups", "heads", "mp", None),
            P("heads", "mp"),
            P("heads", None, "mp"),
        ),
        out_specs=(
            P(None, "groups", ("mp", "heads")),
            P("groups", "heads", "mp", None),
            P("groups", None, "heads", "mp"),
            P("groups", None, None, None, None),
        ),
        check_vma=False,
    )
```

profile of v0, /device:TPU:0, one launch (start us, length us, event | category | flops | bytes accessed | tf_op | source)
XLA Modules:
  0.0 1226.3 jit_solution(14896244926046800657)
XLA Ops:
  57.8 28.5 %all-reduce.39.cloned.1.call-done = (f32[8,2,32,64]{2,3,0,1:T(8,128)}, f32[8,2048]{1,0:T(8,128)}) async-done(((f32[8,2,32,64]{2,3,0,1:T(8,128)}, f32[8,2048]{1,0:T(8,128)}), (f32[8,2,32,64]{2,3,0,1:T(8,128)}, f32[8,2048]{1,0:T(8,128)})) %all-reduce.39.cloned.1.call-update) | async-done | bytes 196624 | tf_op jit(solution)/shard_map/psum | solution.py:62
  92.7 31.1 %psum.284 = f32[8,4]{0,1:T(4,128)S(1)} all-reduce(f32[8,4]{0,1:T(4,128)S(1)} %select_reduce_fusion.31), channel_id=1, replica_groups=mesh['groups'=2,'mp'=4,'heads'=4] {'mp','heads'}, use_global_device_ids=true, to_apply=%region_12.13 | all-reduce | flops 32 | bytes 256 | tf_op jit(solution)/shard_map/psum | solution.py:96
  146.5 16.8 %reduce-scatter.9.cloned.1.call-done = f32[8,512]{1,0:T(8,128)} async-done(((f32[8,2048]{1,0:T(8,128)}), f32[8,512]{1,0:T(8,128)}) %reduce-scatter.9.cloned.1.call-update) | async-done | bytes 16400 | tf_op jit(solution)/shard_map/reduce_scatter | solution.py:108
  198.0 36.8 %all-reduce.37.cloned.1.call-done = (f32[8,2,32,64]{2,3,0,1:T(8,128)}, f32[8,2048]{1,0:T(8,128)}) async-done(((f32[8,2,32,64]{2,3,0,1:T(8,128)}, f32[8,2048]{1,0:T(8,128)}), (f32[8,2,32,64]{2,3,0,1:T(8,128)}, f32[8,2048]{1,0:T(8,128)})) %all-reduce.37.cloned.1.call-update) | async-done | bytes 196624 | tf_op jit(solution)/shard_map/psum | solution.py:62
  242.1 31.1 %psum.289 = f32[8,4]{0,1:T(4,128)S(1)} all-reduce(f32[8,4]{0,1:T(4,128)S(1)} %select_reduce_fusion.29), channel_id=1, replica_groups=mesh['groups'=2,'mp'=4,'heads'=4] {'mp','heads'}, use_global_device_ids=true, to_apply=%region_27.28 | all-reduce | flops 32 | bytes 256 | tf_op jit(solution)/shard_map/psum | solution.py:96
  295.6 16.8 %reduce-scatter.11.cloned.1.call-done = f32[8,512]{1,0:T(8,128)} async-done(((f32[8,2048]{1,0:T(8,128)}), f32[8,512]{1,0:T(8,128)}) %reduce-scatter.11.cloned.1.call-update) | async-done | bytes 16400 | tf_op jit(solution)/shard_map/reduce_scatter | solution.py:108
  347.0 36.8 %all-reduce.35.cloned.1.call-done = (f32[8,2,32,64]{2,3,0,1:T(8,128)}, f32[8,2048]{1,0:T(8,128)}) async-done(((f32[8,2,32,64]{2,3,0,1:T(8,128)}, f32[8,2048]{1,0:T(8,128)}), (f32[8,2,32,64]{2,3,0,1:T(8,128)}, f32[8,2048]{1,0:T(8,128)})) %all-reduce.35.cloned.1.call-update) | async-done | bytes 196624 | tf_op jit(solution)/shard_map/psum | solution.py:62
  393.4 31.1 %psum.294 = f32[8,4]{0,1:T(4,128)S(1)} all-reduce(f32[8,4]{0,1:T(4,128)S(1)} %select_reduce_fusion.27), channel_id=1, replica_groups=mesh['groups'=2,'mp'=4,'heads'=4] {'mp','heads'}, use_global_device_ids=true, to_apply=%region_42.43 | all-reduce | flops 32 | bytes 256 | tf_op jit(solution)/shard_map/psum | solution.py:96
  446.9 16.8 %reduce-scatter.13.cloned.1.call-done = f32[8,512]{1,0:T(8,128)} async-done(((f32[8,2048]{1,0:T(8,128)}), f32[8,512]{1,0:T(8,128)}) %reduce-scatter.13.cloned.1.call-update) | async-done | bytes 16400 | tf_op jit(solution)/shard_map/reduce_scatter | solution.py:108
  498.3 36.8 %all-reduce.33.cloned.1.call-done = (f32[8,2,32,64]{2,3,0,1:T(8,128)}, f32[8,2048]{1,0:T(8,128)}) async-done(((f32[8,2,32,64]{2,3,0,1:T(8,128)}, f32[8,2048]{1,0:T(8,128)}), (f32[8,2,32,64]{2,3,0,1:T(8,128)}, f32[8,2048]{1,0:T(8,128)})) %all-reduce.33.cloned.1.call-update) | async-done | bytes 196624 | tf_op jit(solution)/shard_map/psum | solution.py:62
  546.1 31.1 %psum.299 = f32[8,4]{0,1:T(4,128)S(1)} all-reduce(f32[8,4]{0,1:T(4,128)S(1)} %select_reduce_fusion.25), channel_id=1, replica_groups=mesh['groups'=2,'mp'=4,'heads'=4] {'mp','heads'}, use_global_device_ids=true, to_apply=%region_57.58 | all-reduce | flops 32 | bytes 256 | tf_op jit(solution)/shard_map/psum | solution.py:96
  599.8 16.8 %reduce-scatter.15.cloned.1.call-done = f32[8,512]{1,0:T(8,128)} async-done(((f32[8,2048]{1,0:T(8,128)}), f32[8,512]{1,0:T(8,128)}) %reduce-scatter.15.cloned.1.call-update) | async-done | bytes 16400 | tf_op jit(solution)/shard_map/reduce_scatter | solution.py:108
  651.4 36.8 %all-reduce.31.cloned.1.call-done = (f32[8,2,32,64]{2,3,0,1:T(8,128)}, f32[8,2048]{1,0:T(8,128)}) async-done(((f32[8,2,32,64]{2,3,0,1:T(8,128)}, f32[8,2048]{1,0:T(8,128)}), (f32[8,2,32,64]{2,3,0,1:T(8,128)}, f32[8,2048]{1,0:T(8,128)})) %all-reduce.31.cloned.1.call-update) | async-done | bytes 196624 | tf_op jit(solution)/shard_map/psum | solution.py:62
  694.6 31.1 %psum.304 = f32[8,4]{0,1:T(4,128)S(1)} all-reduce(f32[8,4]{0,1:T(4,128)S(1)} %select_reduce_fusion.23), channel_id=1, replica_groups=mesh['groups'=2,'mp'=4,'heads'=4] {'mp','heads'}, use_global_device_ids=true, to_apply=%region_72.73 | all-reduce | flops 32 | bytes 256 | tf_op jit(solution)/shard_map/psum | solution.py:96
  748.0 16.8 %reduce-scatter.17.cloned.1.call-done = f32[8,512]{1,0:T(8,128)} async-done(((f32[8,2048]{1,0:T(8,128)}), f32[8,512]{1,0:T(8,128)}) %reduce-scatter.17.cloned.1.call-update) | async-done | bytes 16400 | tf_op jit(solution)/shard_map/reduce_scatter | solution.py:108
  799.6 36.8 %all-reduce.29.cloned.1.call-done = (f32[8,2,32,64]{2,3,0,1:T(8,128)}, f32[8,2048]{1,0:T(8,128)}) async-done(((f32[8,2,32,64]{2,3,0,1:T(8,128)}, f32[8,2048]{1,0:T(8,128)}), (f32[8,2,32,64]{2,3,0,1:T(8,128)}, f32[8,2048]{1,0:T(8,128)})) %all-reduce.29.cloned.1.call-update) | async-done | bytes 196624 | tf_op jit(solution)/shard_map/psum | solution.py:62
  843.7 31.1 %psum.309 = f32[8,4]{0,1:T(4,128)S(1)} all-reduce(f32[8,4]{0,1:T(4,128)S(1)} %select_reduce_fusion.21), channel_id=1, replica_groups=mesh['groups'=2,'mp'=4,'heads'=4] {'mp','heads'}, use_global_device_ids=true, to_apply=%region_87.88 | all-reduce | flops 32 | bytes 256 | tf_op jit(solution)/shard_map/psum | solution.py:96
  897.2 16.8 %reduce-scatter.19.cloned.1.call-done = f32[8,512]{1,0:T(8,128)} async-done(((f32[8,2048]{1,0:T(8,128)}), f32[8,512]{1,0:T(8,128)}) %reduce-scatter.19.cloned.1.call-update) | async-done | bytes 16400 | tf_op jit(solution)/shard_map/reduce_scatter | solution.py:108
  948.8 36.8 %all-reduce.27.cloned.1.call-done = (f32[8,2,32,64]{2,3,0,1:T(8,128)}, f32[8,2048]{1,0:T(8,128)}) async-done(((f32[8,2,32,64]{2,3,0,1:T(8,128)}, f32[8,2048]{1,0:T(8,128)}), (f32[8,2,32,64]{2,3,0,1:T(8,128)}, f32[8,2048]{1,0:T(8,128)})) %all-reduce.27.cloned.1.call-update) | async-done | bytes 196624 | tf_op jit(solution)/shard_map/psum | solution.py:62
  995.1 31.1 %psum.314 = f32[8,4]{0,1:T(4,128)S(1)} all-reduce(f32[8,4]{0,1:T(4,128)S(1)} %select_reduce_fusion.19), channel_id=1, replica_groups=mesh['groups'=2,'mp'=4,'heads'=4] {'mp','heads'}, use_global_device_ids=true, to_apply=%region_102.103 | all-reduce | flops 32 | bytes 256 | tf_op jit(solution)/shard_map/psum | solution.py:96
  1048.8 16.8 %reduce-scatter.21.cloned.1.call-done = f32[8,512]{1,0:T(8,128)} async-done(((f32[8,2048]{1,0:T(8,128)}), f32[8,512]{1,0:T(8,128)}) %reduce-scatter.21.cloned.1.call-update) | async-done | bytes 16400 | tf_op jit(solution)/shard_map/reduce_scatter | solution.py:108
  1100.3 36.8 %all-reduce.25.cloned.1.call-done = (f32[8,2,32,64]{2,3,0,1:T(8,128)}, f32[8,2048]{1,0:T(8,128)}) async-done(((f32[8,2,32,64]{2,3,0,1:T(8,128)}, f32[8,2048]{1,0:T(8,128)}), (f32[8,2,32,64]{2,3,0,1:T(8,128)}, f32[8,2048]{1,0:T(8,128)})) %all-reduce.25.cloned.1.call-update) | async-done | bytes 196624 | tf_op jit(solution)/shard_map/psum | solution.py:62
  1148.1 31.1 %psum.319 = f32[8,4]{0,1:T(4,128)S(1)} all-reduce(f32[8,4]{0,1:T(4,128)S(1)} %select_reduce_fusion.17), channel_id=1, replica_groups=mesh['groups'=2,'mp'=4,'heads'=4] {'mp','heads'}, use_global_device_ids=true, to_apply=%region_117.118 | all-reduce | flops 32 | bytes 256 | tf_op jit(solution)/shard_map/psum | solution.py:96
  1202.8 15.5 %reduce-scatter.23.cloned.1.call-done = f32[8,512]{1,0:T(8,128)} async-done(((f32[8,2048]{1,0:T(8,128)}), f32[8,512]{1,0:T(8,128)}) %reduce-scatter.23.cloned.1.call-update) | async-done | bytes 16400 | tf_op jit(solution)/shard_map/reduce_scatter | solution.py:108
  (332 shorter events, 543.1 us)
Async XLA Ops:
  7.2 37.7 %copy-start = (bf16[2048,32]{0,1:T(8,128)(2,1)S(1)}, bf16[2048,32]{0,1:T(8,128)(2,1)}, u32[]{:S(2)}) copy-start(bf16[2048,32]{0,1:T(8,128)(2,1)} %param.19) | copy-start | bytes 393220
  7.2 79.1 %all-reduce.39.cloned.1.call-start = ((), (), s32[]{:S(2)}) async-start(), calls=%async_computation.23 | async-start | bytes 1179648 | tf_op jit(solution)/shard_map/psum | solution.py:62
  39.3 18.4 %copy-start.9 = (f32[32]{0:T(128)S(1)}, f32[32]{0:T(128)}, u32[]{:S(2)}) copy-start(f32[32]{0:T(128)} %param.20) | copy-start | bytes 388
  39.3 48.9 %copy-start.2 = (f32[4,32,16]{1,2,0:T(8,128)S(1)}, f32[4,32,16]{1,2,0:T(8,128)}, u32[]{:S(2)}) copy-start(f32[4,32,16]{1,2,0:T(8,128)} %param.23) | copy-start | bytes 24580
  39.3 48.9 %copy-start.5 = (bf16[8,3,32,16]{2,3,1,0:T(8,128)(2,1)S(1)}, bf16[8,3,32,16]{2,3,1,0:T(8,128)(2,1)}, u32[]{:S(2)}) copy-start(bf16[8,3,32,16]{2,3,1,0:T(8,128)(2,1)} %param.25) | copy-start | bytes 73732
  39.3 49.1 %copy-start.3 = (f32[4,2,4,256]{3,2,1,0:T(4,128)S(1)}, f32[4,2,4,256]{3,2,1,0:T(4,128)}, u32[]{:S(2)}) copy-start(f32[4,2,4,256]{3,2,1,0:T(4,128)} %param.24) | copy-start | bytes 98308
  44.6 47.9 %copy-start.7 = (f32[32]{0:T(128)S(1)}, f32[32]{0:T(128)}, u32[]{:S(2)}) copy-start(f32[32]{0:T(128)} %param.22) | copy-start | bytes 388
  44.6 79.2 %copy-start.4 = (f32[32,16]{0,1:T(8,128)S(1)}, f32[32,16]{0,1:T(8,128)}, u32[]{:S(2)}) copy-start(f32[32,16]{0,1:T(8,128)} %param.28) | copy-start | bytes 6148
  44.7 118.6 %reduce-scatter.9.cloned.1.call-start = ((), (), s32[]{:S(2)}) async-start(), calls=%async_computation.8 | async-start | bytes 81920 | tf_op jit(solution)/shard_map/reduce_scatter | solution.py:108
  137.8 25.4 %copy-start.10 = (bf16[8,512]{1,0:T(8,128)(2,1)S(1)}, bf16[8,512]{1,0:T(8,128)(2,1)}, u32[]{:S(2)}) copy-start(bf16[8,512]{1,0:T(8,128)(2,1)} %param.15) | copy-start | bytes 24580
  146.3 88.4 %all-reduce.37.cloned.1.call-start = ((), (), s32[]{:S(2)}) async-start(), calls=%async_computation.22 | async-start | bytes 1179648 | tf_op jit(solution)/shard_map/psum | solution.py:62
  197.8 114.5 %reduce-scatter.11.cloned.1.call-start = ((), (), s32[]{:S(2)}) async-start(), calls=%async_computation.9 | async-start | bytes 81920 | tf_op jit(solution)/shard_map/reduce_scatter | solution.py:108
  295.4 88.4 %all-reduce.35.cloned.1.call-start = ((), (), s32[]{:S(2)}) async-start(), calls=%async_computation.21 | async-start | bytes 1179648 | tf_op jit(solution)/shard_map/psum | solution.py:62
  346.9 116.7 %reduce-scatter.13.cloned.1.call-start = ((), (), s32[]{:S(2)}) async-start(), calls=%async_computation.10 | async-start | bytes 81920 | tf_op jit(solution)/shard_map/reduce_scatter | solution.py:108
  446.7 88.4 %all-reduce.33.cloned.1.call-start = ((), (), s32[]{:S(2)}) async-start(), calls=%async_computation.20 | async-start | bytes 1179648 | tf_op jit(solution)/shard_map/psum | solution.py:62
  498.2 118.4 %reduce-scatter.15.cloned.1.call-start = ((), (), s32[]{:S(2)}) async-start(), calls=%async_computation.11 | async-start | bytes 81920 | tf_op jit(solution)/shard_map/reduce_scatter | solution.py:108
  599.7 88.5 %all-reduce.31.cloned.1.call-start = ((), (), s32[]{:S(2)}) async-start(), calls=%async_computation.19 | async-start | bytes 1179648 | tf_op jit(solution)/shard_map/psum | solution.py:62
  651.2 113.6 %reduce-scatter.17.cloned.1.call-start = ((), (), s32[]{:S(2)}) async-start(), calls=%async_computation.12 | async-start | bytes 81920 | tf_op jit(solution)/shard_map/reduce_scatter | solution.py:108
  747.9 88.5 %all-reduce.29.cloned.1.call-start = ((), (), s32[]{:S(2)}) async-start(), calls=%async_computation.18 | async-start | bytes 1179648 | tf_op jit(solution)/shard_map/psum | solution.py:62
  799.4 114.6 %reduce-scatter.19.cloned.1.call-start = ((), (), s32[]{:S(2)}) async-start(), calls=%async_computation.13 | async-start | bytes 81920 | tf_op jit(solution)/shard_map/reduce_scatter | solution.py:108
  897.1 88.5 %all-reduce.27.cloned.1.call-start = ((), (), s32[]{:S(2)}) async-start(), calls=%async_computation.17 | async-start | bytes 1179648 | tf_op jit(solution)/shard_map/psum | solution.py:62
  948.6 116.9 %reduce-scatter.21.cloned.1.call-start = ((), (), s32[]{:S(2)}) async-start(), calls=%async_computation.14 | async-start | bytes 81920 | tf_op jit(solution)/shard_map/reduce_scatter | solution.py:108
  1048.6 88.4 %all-reduce.25.cloned.1.call-start = ((), (), s32[]{:S(2)}) async-start(), calls=%async_computation.16 | async-start | bytes 1179648 | tf_op jit(solution)/shard_map/psum | solution.py:62
  1100.1 118.1 %reduce-scatter.23.cloned.1.call-start = ((), (), s32[]{:S(2)}) async-start(), calls=%async_computation.15 | async-start | bytes 81920 | tf_op jit(solution)/shard_map/reduce_scatter | solution.py:108
  (4 other events, 51.7 us)
Sparse Core Ops, SparseCore 0:
  44.8 41.4 all-reduce.38
  146.5 16.7 reduce-scatter.8
  197.9 36.7 all-reduce.36
  295.5 16.7 reduce-scatter.10
  347.0 36.7 all-reduce.34
  446.8 16.7 reduce-scatter.12
  498.3 36.7 all-reduce.32
  599.8 16.7 reduce-scatter.14
  651.4 36.7 all-reduce.30
  748.0 16.7 reduce-scatter.16
  799.6 36.7 all-reduce.28
  897.2 16.7 reduce-scatter.18
  948.8 36.7 all-reduce.26
  1048.8 16.7 reduce-scatter.20
  1100.3 36.7 all-reduce.24
  1201.5 16.7 reduce-scatter.22
where the time goes:
time: 1240 us; the launch traced here: 1230 us
  blocking collectives  496 us (40%)
  waiting for transfers between devices  419 us (34%)
  matrix products  192 us (15%)
  other arithmetic  76.8 us (6%)
  local copies, waits for them, and re-layouts  25.9 us (2%)
  between operations  15.3 us (1%)
    psum x8, waiting for transfers between devices, body(): lax.psum((part_inner, part_state, part_step, part_sq), 'mp')  286 us
    psum x8, blocking collectives, body(): group_total = lax.psum(group_part, ('mp', 'heads'))  249 us
    reduce_scatter x8, waiting for transfers between devices, body(): lax.psum_scatter(partial_out, 'heads', scatter_dimension=1, tiled=True)  133 us
    all_gather x8, blocking collectives, body(): lax.all_gather(normed, 'mp', axis=2, tiled=True)  109 us
    psum x8, blocking collectives, body(): lax.psum((part_inner, part_state, part_step, part_sq), 'mp')  95.2 us
    dot_general x8, matrix products, body(): part_inner = jnp.dot(scaled, flat_inner, preferred_element_type=jnp.float32)  81.6 us
    dot_general x8, matrix products, body(): jnp.einsum('rhp,hpd->rd', lax.all_gather(normed, 'mp', axis=2, tiled=True...  67.8 us
    reduce_sum x8, other arithmetic, body(): jnp.sum(hidden * head_c[:, :, None, :], axis=3)  46.4 us
  transfers between devices with their start and end apart: 16, of which 16 were waited for; matrix products, arithmetic and copies ran while one was open for 0% of the time, Pallas kernels for 0%

commit v1 on v0

--- a/solution.py
+++ b/solution.py
@@ -1,6 +1,10 @@
+import functools
+
 import jax
 import jax.numpy as jnp
 from jax import lax
+from jax.experimental import pallas as pl
+from jax.experimental.pallas import tpu as pltpu
 from jax.sharding import PartitionSpec as P
 
 D = 8192
@@ -111,9 +115,412 @@
     return (jnp.stack(written), hidden, hist_inner, hist_state)
 
 
+LANES = 128
+MESH = pl.DeviceIdType.MESH
+
+
+def silu(v):
+    return v / (1.0 + jnp.exp(-v))
+
+
+def fused_kernel(
+    n_mp,
+    n_heads,
+    n_local,
+    per_head,
+    x_ref,
+    gain_ref,
+    perm_ref,
+    spread_ref,
+    bias_ref,
+    decay_ref,
+    skip_ref,
+    norm_ref,
+    conv_x_ref,
+    conv_bc_ref,
+    hist_x_in,
+    hist_bc_in,
+    w_inner_hbm,
+    w_aux_hbm,
+    w_out_hbm,
+    state_hbm,
+    out_ref,
+    hidden,
+    hist_x,
+    hist_all,
+    w_in,
+    w_aux,
+    w_o,
+    current,
+    gathered,
+    acc,
+    parts,
+    part_in,
+    norm_out,
+    norm_in,
+    out_parts,
+    out_in,
+    hist_bc,
+    hist_in,
+    reading_s,
+    load_sem,
+    send_sem,
+    recv_sem,
+):
+    mi = lax.axis_index("mp")
+    hi = lax.axis_index("heads")
+    rows, feat = x_ref.shape
+    chan = norm_ref.shape[1]
+    part = w_o.shape[2]
+    block = perm_ref.shape[0]
+    n_blocks = w_in.shape[2] // block
+    n_state = w_aux.shape[2] - LANES
+    state_size = n_state // 2
+
+    loads_in = []
+    for d in range(n_heads):
+        owner = lax.rem(hi - d + n_heads, n_heads)
+        span = pl.ds(pl.multiple_of(owner * feat, feat), feat)
+        a = pltpu.make_async_copy(w_inner_hbm.at[span], w_in.at[d], load_sem.at[0, d])
+        b = pltpu.make_async_copy(w_aux_hbm.at[span], w_aux.at[d], load_sem.at[1, d])
+        a.start()
+        loads_in.append((a, b))
+    for a, b in loads_in:
+        b.start()
+    loads_rest = [pltpu.make_async_copy(state_hbm, hidden, load_sem.at[2, 0])]
+    for d in range(n_mp):
+        owner = lax.rem(mi - d + n_mp, n_mp)
+        span = pl.ds(pl.multiple_of(owner * part, part), part)
+        loads_rest.append(
+            pltpu.make_async_copy(w_out_hbm.at[:, span], w_o.at[d], load_sem.at[3, d])
+        )
+    for c in loads_rest:
+        c.start()
+
+    barrier = pltpu.get_barrier_semaphore()
+    for d in range(1, n_heads):
+        pl.semaphore_signal(
+            barrier,
+            inc=1,
+            device_id={"heads": lax.rem(hi + d, n_heads)},
+            device_id_type=MESH,
+        )
+    for d in range(1, n_mp):
+        pl.semaphore_signal(
+            barrier, inc=1, device_id={"mp": lax.rem(mi + d, n_mp)}, device_id_type=MESH
+        )
+    pl.semaphore_wait(barrier, n_heads + n_mp - 2)
+
+    current[...] = x_ref[...]
+    hist_x[...] = hist_x_in[...]
+    hist_bc[...] = hist_bc_in[...]
+
+    row_chunk = min(feat, 256)
+    for d in range(n_heads):
+        loads_in[d][0].wait()
+
+        @pl.loop(0, n_blocks)
+        def _(b):
+            cols = pl.ds(pl.multiple_of(b * block, block), block)
+            for r in range(0, feat, row_chunk):
+                moved = jnp.dot(
+                    w_in[d, r : r + row_chunk, cols],
+                    perm_ref[...],
+                    preferred_element_type=jnp.float32,
+                )
+                w_in[d, r : r + row_chunk, cols] = moved.astype(jnp.bfloat16)
+
+    for a, b in loads_in:
+        b.wait()
+    for c in loads_rest:
+        c.wait()
+
+    def exchange(phase, axis, me, n, source, dest):
+        copies = []
+        for d in range(1, n):
+            target = lax.rem(me + d, n)
+            c = pltpu.make_async_remote_copy(
+                src_ref=source(target),
+                dst_ref=dest.at[d],
+                send_sem=send_sem.at[phase, d],
+                recv_sem=recv_sem.at[phase, d],
+                device_id={axis: target},
+                device_id_type=MESH,
+            )
+            c.start()
+            copies.append(c)
+        return copies
+
+    chunk = block
+
+    def step(s, carry):
+        cur = current[...]
+        sent = exchange(0, "heads", hi, n_heads, lambda t: current, gathered)
+        first = (cur * gain_ref[hi]).astype(jnp.bfloat16)
+        sq = jnp.sum(cur * cur, axis=1, keepdims=True)
+        for b in range(n_blocks):
+            lo = b * chunk
+            acc[:, lo : lo + chunk] = jnp.dot(
+                first, w_in[0, :, lo : lo + chunk], preferred_element_type=jnp.float32
+            )
+        aux = jnp.dot(first, w_aux[0], preferred_element_type=jnp.float32)
+        later = []
+        for d in range(1, n_heads):
+            sent[d - 1].wait()
+            v = gathered[d]
+            owner = lax.rem(hi - d + n_heads, n_heads)
+            later.append((v * gain_ref[owner]).astype(jnp.bfloat16))
+            sq = sq + jnp.sum(v * v, axis=1, keepdims=True)
+        for b in range(n_blocks):
+            lo = b * chunk
+            total = acc[:, lo : lo + chunk]
+            for d in range(1, n_heads):
+                total = total + jnp.dot(
+                    later[d - 1],
+                    w_in[d, :, lo : lo + chunk],
+                    preferred_element_type=jnp.float32,
+                )
+            for m in range(n_mp):
+                parts[m, :, b * LANES : (b + 1) * LANES] = total[:, m * LANES : (m + 1) * LANES]
+        for d in range(1, n_heads):
+            aux = aux + jnp.dot(later[d - 1], w_aux[d], preferred_element_type=jnp.float32)
+        lane = lax.broadcasted_iota(jnp.int32, (rows, LANES), 1)
+        tail = jnp.where(lane == n_local, sq, aux[:, n_state:])
+        for m in range(n_mp):
+            parts[m, :, 2 * chan : 2 * chan + n_state] = aux[:, :n_state]
+            parts[m, :, 2 * chan + n_state :] = tail
+
+        sent = exchange(1, "mp", mi, n_mp, lambda t: parts.at[t], part_in)
+        total = parts[mi]
+        for d in range(1, n_mp):
+            sent[d - 1].wait()
+            total = total + part_in[d]
+        tail = total[:, 2 * chan + n_state :]
+        inv = lax.rsqrt(tail[:, n_local : n_local + 1] / D + EPSILON)
+        new_x = (total[:, :chan] * inv).astype(jnp.bfloat16).astype(jnp.float32)
+        gate = total[:, chan : 2 * chan] * inv
+        new_bc = (
+            (total[:, 2 * chan : 2 * chan + n_state] * inv)
+            .astype(jnp.bfloat16)
+            .astype(jnp.float32)
+        )
+
+        def conv(hist, new, kernel):
+            old = [hist[0], hist[1], hist[2]]
+            hist[0] = old[1]
+            hist[1] = old[2]
+            hist[2] = new
+            v = old[0] * kernel[0] + old[1] * kernel[1] + old[2] * kernel[2] + new * kernel[3]
+            return silu(v)
+
+        conv_x = conv(hist_x, new_x, conv_x_ref)
+        conv_bc = conv(hist_bc, new_bc, conv_bc_ref)
+        spread = jnp.dot(
+            tail,
+            spread_ref[...],
+            preferred_element_type=jnp.float32,
+            precision=lax.Precision.HIGHEST,
+        )
+        raw = spread * inv + bias_ref[...]
+        dt = jnp.maximum(raw, 0.0) + jnp.log1p(jnp.exp(-jnp.abs(raw)))
+        decay = jnp.exp(-dt * decay_ref[...])
+        driven = dt * conv_x
+        b_cols = jnp.transpose(conv_bc[:, :state_size])
+        c_cols = jnp.transpose(conv_bc[:, state_size:])
+        part_n = min(state_size, 64)
+        for r in range(rows):
+            sums = [jnp.zeros((part_n, LANES), jnp.float32) for _ in range(chan // LANES)]
+            for n0 in range(0, state_size, part_n):
+                b_wide = jnp.broadcast_to(b_cols[n0 : n0 + part_n, r : r + 1], (part_n, LANES))
+                c_wide = jnp.broadcast_to(c_cols[n0 : n0 + part_n, r : r + 1], (part_n, LANES))
+                for c in range(chan // LANES):
+                    cols = slice(c * LANES, (c + 1) * LANES)
+                    h = (
+                        decay[r : r + 1, cols] * hidden[r, n0 : n0 + part_n, cols]
+                        + driven[r : r + 1, cols] * b_wide
+                    )
+                    hidden[r, n0 : n0 + part_n, cols] = h
+                    sums[c] = sums[c] + h * c_wide
+            for c in range(chan // LANES):
+                reading_s[r : r + 1, c * LANES : (c + 1) * LANES] = jnp.sum(
+                    sums[c], axis=0, keepdims=True
+                )
+        reading = reading_s[...] + skip_ref[...] * conv_x
+        gated = reading * silu(gate)
+        group_sq = jnp.sum(gated * gated, axis=1, keepdims=True)
+        mine = (gated * norm_ref[...]).astype(jnp.bfloat16)
+        norm_out[:, :chan] = mine.astype(jnp.float32)
+        norm_out[:, chan:] = jnp.broadcast_to(group_sq, (rows, LANES))
+
+        sent = exchange(2, "mp", mi, n_mp, lambda t: norm_out, norm_in)
+
+        def out_weight(d, b):
+            w = w_o[d, :, :, b * feat : (b + 1) * feat]
+            return w.reshape(w.shape[0] * w.shape[1], feat)
+
+        for b in range(n_heads):
+            out_parts[b] = jnp.dot(mine, out_weight(0, b), preferred_element_type=jnp.float32)
+        later = []
+        for d in range(1, n_mp):
+            sent[d - 1].wait()
+            later.append(norm_in[d, :, :chan].astype(jnp.bfloat16))
+            group_sq = group_sq + norm_in[d, :, chan : chan + 1]
+        scale = lax.rsqrt(group_sq / (n_local * per_head) + EPSILON)
+        for b in range(n_heads):
+            total = out_parts[b]
+            for d in range(1, n_mp):
+                total = total + jnp.dot(
+                    later[d - 1], out_weight(d, b), preferred_element_type=jnp.float32
+                )
+            out_parts[b] = total * scale
+
+        sent = exchange(3, "heads", hi, n_heads, lambda t: out_parts.at[t], out_in)
+        update = out_parts[hi]
+        for d in range(1, n_heads):
+            sent[d - 1].wait()
+            update = update + out_in[d]
+        new = (cur + update).astype(jnp.bfloat16).astype(jnp.float32)
+        current[...] = new
+        out_ref[s] = new
+        return carry
+
+    lax.fori_loop(0, STEPS, step, 0)
+
+    sent = exchange(4, "heads", hi, n_heads, lambda t: hist_bc, hist_in)
+    hist_all[hi] = hist_bc[...]
+    for d in range(1, n_heads):
+        sent[d - 1].wait()
+        hist_all[lax.rem(hi - d + n_heads, n_heads)] = hist_in[d]
+
+
+def fused_body(
+    n_mp,
+    n_heads,
+    stream,
+    in_gain,
+    w_inner,
+    w_state,
+    w_step,
+    step_bias,
+    decay_scale,
+    skip_gain,
+    conv_inner,
+    conv_state_weight,
+    history_inner,
+    history_state,
+    ssm_state,
+    norm_gain,
+    w_out,
+):
+    f32, bf16 = jnp.float32, jnp.bfloat16
+    rows, feat = stream.shape
+    width, _, n_local, per_head = w_inner.shape
+    part = ssm_state.shape[2]
+    state_size = w_state.shape[3]
+    n_groups = w_state.shape[2]
+    chan = n_local * part
+    n_state = 2 * state_size
+    hi = lax.axis_index("heads")
+    in_block = LANES // part
+    block = in_block * per_head
+    i_in = jnp.arange(block)
+    head, slot, lane = i_in // per_head, (i_in % per_head) // part, i_in % part
+    place = slot * LANES + head * part + lane
+    perm = (place[:, None] == jnp.arange(block)[None, :]).astype(bf16)
+    spread = (jnp.arange(LANES)[:, None] == (jnp.arange(chan) // part)[None, :]).astype(f32)
+    own_state = lax.dynamic_slice_in_dim(w_state, hi, 1, 2).reshape(width, n_state)
+    aux = jnp.concatenate([own_state, jnp.pad(w_step, ((0, 0), (0, LANES - n_local)))], axis=1)
+    wide = lambda v: jnp.repeat(v, part)[None]
+    own_conv = lax.dynamic_slice_in_dim(conv_state_weight, hi, 1, 2).reshape(4, 1, n_state)
+    own_hist = lax.dynamic_slice_in_dim(history_state, hi, 1, 3).reshape(rows, 3, n_state)
+    vmem = pl.BlockSpec(memory_space=pltpu.VMEM)
+    hbm = pl.BlockSpec(memory_space=pl.ANY)
+    shape = jax.ShapeDtypeStruct
+    out, hidden, hist_x, hist_bc = pl.pallas_call(
+        functools.partial(fused_kernel, n_mp, n_heads, n_local, per_head),
+        out_shape=(
+            shape((STEPS, rows, feat), f32),
+            shape((rows, state_size, chan), f32),
+            shape((3, rows, chan), f32),
+            shape((n_heads, 3, rows, n_state), f32),
+        ),
+        in_specs=[vmem] * 12 + [hbm] * 4,
+        out_specs=(vmem,) * 4,
+        scratch_shapes=[
+            pltpu.VMEM((n_heads, feat, 2 * n_local * per_head), bf16),
+            pltpu.VMEM((n_heads, feat, n_state + LANES), bf16),
+            pltpu.VMEM((n_mp, n_local, part, w_out.shape[2]), bf16),
+            pltpu.VMEM((rows, feat), f32),
+            pltpu.VMEM((n_heads, rows, feat), f32),
+            pltpu.VMEM((rows, 2 * n_local * per_head), f32),
+            pltpu.VMEM((n_mp, rows, 2 * chan + n_state + LANES), f32),
+            pltpu.VMEM((n_mp, rows, 2 * chan + n_state + LANES), f32),
+            pltpu.VMEM((rows, chan + LANES), f32),
+            pltpu.VMEM((n_mp, rows, chan + LANES), f32),
+            pltpu.VMEM((n_heads, rows, feat), f32),
+            pltpu.VMEM((n_heads, rows, feat), f32),
+            pltpu.VMEM((3, rows, n_state), f32),
+            pltpu.VMEM((n_heads, 3, rows, n_state), f32),
+            pltpu.VMEM((rows, chan), f32),
+            pltpu.SemaphoreType.DMA((4, max(n_mp, n_heads))),
+            pltpu.SemaphoreType.DMA((5, max(n_mp, n_heads))),
+            pltpu.SemaphoreType.DMA((5, max(n_mp, n_heads))),
+        ],
+        compiler_params=pltpu.CompilerParams(
+            collective_id=0, has_side_effects=True, vmem_limit_bytes=56 * 1024 * 1024
+        ),
+    )(
+        stream.astype(f32),
+        in_gain.reshape(n_heads, 1, feat),
+        perm,
+        spread,
+        wide(step_bias),
+        wide(decay_scale),
+        wide(skip_gain),
+        norm_gain.reshape(1, chan),
+        conv_inner.reshape(4, 1, chan),
+        own_conv,
+        jnp.swapaxes(history_inner.reshape(rows, 3, chan), 0, 1).astype(f32),
+        jnp.swapaxes(own_hist, 0, 1).astype(f32),
+        w_inner.reshape(width, 2 * n_local * per_head),
+        aux,
+        w_out,
+        jnp.swapaxes(ssm_state.reshape(rows, chan, state_size), 1, 2),
+    )
+    hist_bc = hist_bc.reshape(n_groups, 3, rows, 2, state_size).transpose(2, 1, 3, 0, 4)
+    return (
+        out.astype(bf16),
+        jnp.swapaxes(hidden, 1, 2).reshape(ssm_state.shape),
+        jnp.swapaxes(hist_x, 0, 1).reshape(history_inner.shape).astype(bf16),
+        hist_bc.astype(bf16),
+    )
+
+
+def choose_body(n_mp, n_heads):
+    def run(*args):
+        stream, w_inner, w_state, ssm_state = args[0], args[2], args[3], args[12]
+        n_local, per_head = w_inner.shape[2], w_inner.shape[3]
+        part = ssm_state.shape[2]
+        aligned = (
+            n_local == NH // NG
+            and n_heads == w_state.shape[2]
+            and n_local < LANES
+            and LANES % part == 0
+            and per_head == part * n_mp
+            and (n_local * part) % LANES == 0
+            and stream.shape[1] % LANES == 0
+            and w_state.shape[3] % LANES == 0
+        )
+        if aligned:
+            return fused_body(n_mp, n_heads, *args)
+        return body(*args)
+
+    return run
+
+
 def solution(mesh):
     return jax.shard_map(
-        body,
+        choose_body(mesh.shape["mp"], mesh.shape["heads"]),
         mesh=mesh,
         in_specs=(
             P("groups", ("mp", "heads")),

time: 1240 us -> 263 us (0.21)
  blocking collectives: 496 us -> 0 us
  waiting for transfers between devices: 419 us -> 0 us
  matrix products: 192 us -> 0 us
  Pallas kernels: 0 us -> 188 us
  other arithmetic: 76.8 us -> 8.58 us
  local copies, waits for them, and re-layouts: 25.9 us -> 64.1 us
  between operations: 15.3 us -> 0.74 us
    psum x16 -> x0, blocking collectives: 344 us -> none  [the longest x8 249 us: body(): group_total = lax.psum(group_part, ('mp', 'heads'))]
    psum x8 -> x0, waiting for transfers between devices: 286 us -> none  [body(): lax.psum((part_inner, part_state, part_step, part_sq), 'mp')]
    dot_general x32 -> x0, matrix products: 192 us -> none  [the longest x8 81.6 us: body(): part_inner = jnp.dot(scaled, flat_inner, preferred_element_type=jnp.float32)]
    pallas_call x0 -> x1, Pallas kernels: none -> 188 us  [fused_body(): pl.pallas_call(functools.partial(fused_kernel, n_mp, n_heads, n_local, pe...]
    all_gather x16 -> x0, blocking collectives: 152 us -> none  [the longest x8 109 us: body(): lax.all_gather(normed, 'mp', axis=2, tiled=True)]
    reduce_scatter x8 -> x0, waiting for transfers between devices: 133 us -> none  [body(): lax.psum_scatter(partial_out, 'heads', scatter_dimension=1, tiled=True)]
    reduce_sum x64 -> x0, other arithmetic: 52.3 us -> none  [the longest x8 46.4 us: body(): jnp.sum(hidden * head_c[:, :, None, :], axis=3)]
    reshape x17 -> x5, local copies, waits for them, and re-layouts: 23.5 us -> 30.6 us  [the longest x1 21.4 us: fused_body(): w_inner.reshape(width, 2 * n_local * per_head)]
  transfers between devices with their start and end apart: 16 -> 0, of which waited for: 16 -> 0; matrix products, arithmetic and copies ran while one was open for 0% -> 0% of each run, Pallas kernels for 0% -> 0%
where the time goes in v1:
time: 263 us; the launch traced here: 261 us
  Pallas kernels  188 us (71%)
  local copies, waits for them, and re-layouts  64.1 us (24%)
  other arithmetic  8.58 us (3%)
    pallas_call x1, Pallas kernels, fused_body(): pl.pallas_call(functools.partial(fused_kernel, n_mp, n_heads, n_local, pe...  188 us
    reshape x1, local copies, waits for them, and re-layouts, fused_body(): w_inner.reshape(width, 2 * n_local * per_head)  21.4 us
    unnamed x14, local copies, waits for them, and re-layouts  12.6 us
    dynamic_slice x1, local copies, waits for them, and re-layouts, fused_body(): lax.dynamic_slice_in_dim(w_state, hi, 1, 2).reshape(width, n_state)  7.26 us
    transpose x1, local copies, waits for them, and re-layouts, fused_body(): jnp.swapaxes(hidden, 1, 2).reshape(ssm_state.shape)  5.39 us
    reshape x1, local copies, waits for them, and re-layouts, fused_body(): ssm_state.reshape(rows, chan, state_size)  5.34 us

profile of v1, /device:TPU:0, one launch (start us, length us, event | category | flops | bytes accessed | tf_op | source)
XLA Modules:
  0.0 261.5 jit_solution(7317284613505835430)
XLA Ops:
  0.7 1.4 constant_dynamic-slice_fusion.2
  2.0 1.3 convert_element_type.46.x_ref
  3.3 0.7 broadcast_in_dim.6
  4.7 0.7 broadcast_in_dim.14
  6.1 0.7 broadcast_in_dim.15
  7.5 0.8 copy.42
  9.6 0.8 copy.43
  10.5 0.7 reshape.113.conv_x_ref
  11.2 0.7 fusion.3.spread_ref
  11.9 1.0 copy.44
  12.9 0.8 reshape.111
  13.7 1.0 fusion.2.perm_ref
  14.7 1.2 copy.48
  15.9 7.3 %constant_dynamic-slice_fusion = bf16[2048,2,1,256]{3,2,1,0:T(2,128)(2,1)} fusion(bf16[2048,2,4,256]{3,2,1,0:T(4,128)(2,1)} %param.18, s32[]{:T(128)S(6)} %select_n.52), kind=kLoop, calls=%fused_computation.38 | loop fusion | bytes 4194308 | tf_op jit(solution)/shard_map/dynamic_slice | solution.py:431
  23.1 9.0 %copy.57 = bf16[2048,2,1,256]{0,3,1,2:T(8,128)(2,1)S(1)} copy(bf16[2048,2,1,256]{3,2,1,0:T(2,128)(2,1)} %constant_dynamic-slice_fusion) | data formatting | bytes 4194304
  32.2 2.5 copy.49
  34.7 3.4 %fusion.1.w_aux_hbm = bf16[2048,640]{1,0:T(8,128)(2,1)} fusion(bf16[2048,32]{1,0:T(8,128)(2,1)S(1)} %copy.48, bf16[2048,512]{1,0:T(8,128)(2,1)} %copy.49), kind=kLoop, calls=%fused_computation.2 | loop fusion | flops 7864320 | bytes 4849664 | tf_op jit(solution)/shard_map/concatenate | solution.py:432
  38.0 5.3 %copy.50 = f32[8,512,256]{1,2,0:T(8,128)} copy(f32[8,512,256]{2,1,0:T(8,128)} %bitcast.31) | data formatting | bytes 8388608 | tf_op jit(solution)/shard_map/reshape | solution.py:488
  43.4 21.4 %copy.52.w_inner_hbm = bf16[2048,4096]{1,0:T(8,128)(2,1)} copy(bf16[2048,4096]{0,1:T(8,128)(2,1)} %bitcast.29) | data formatting | bytes 33554432 | tf_op jit(solution)/shard_map/reshape | solution.py:485
  64.8 188.1 %shard_map.174 = (f32[8,8,512]{2,1,0:T(8,128)}, f32[8,256,512]{2,1,0:T(8,128)}, f32[3,8,512]{2,1,0:T(8,128)}, f32[4,3,8,512]{3,2,1,0:T(8,128)}) custom-call(f32[8,512]{1,0:T(8,128)} %convert_element_type.46.x_ref, f32[4,1,512]{2,1,0:T(1,128)} %bitcast.39, bf16[512,512]{1,0:T(8,128)(2,1)} %fusion.2.perm_ref, f32[128,512]{1,0:T(8,128)} %fusion.3.spread_ref, ...), custom_call_target="tpu_custom_call" | custom-call | tf_op jit(solution)/shard_map/pallas_call | solution.py:439
  252.9 1.5 convert_element_type.55
  254.4 5.4 %copy.53 = f32[8,512,256]{2,1,0:T(8,128)} copy(f32[8,512,256]{1,2,0:T(8,128)} %bitcast.33) | data formatting | bytes 8388608 | tf_op jit(solution)/shard_map/transpose | solution.py:493
  259.8 0.7 copy.59
  260.7 0.8 copy.55
  (20 shorter events, 3.6 us)
Async XLA Ops:
  0.6 8.3 %copy-start = (bf16[8,3,2,4,256]{4,3,2,1,0:T(4,128)(2,1)S(1)}, bf16[8,3,2,4,256]{4,3,2,1,0:T(4,128)(2,1)}, u32[]{:S(2)}) copy-start(bf16[8,3,2,4,256]{4,3,2,1,0:T(4,128)(2,1)} %param.26) | copy-start | bytes 294916
  254.4 7.1 %copy-start.1 = (bf16[8,3,2,4,256]{4,3,2,1,0:T(4,128)(2,1)S(1)}, bf16[8,3,2,4,256]{4,3,2,1,0:T(4,128)(2,1)}, u32[]{:S(2)}) copy-start(bf16[8,3,2,4,256]{4,3,2,1,0:T(4,128)(2,1)} %param.26) | copy-start | bytes 294916
  254.4 5.4 %copy-start.3 = (f32[3,8,512]{2,1,0:T(8,128)S(1)}, f32[3,8,512]{2,1,0:T(8,128)}, u32[]{:S(2)}) copy-start(f32[3,8,512]{2,1,0:T(8,128)} %get-tuple-element.10) | copy-start | bytes 147460
  254.4 5.4 %copy-start.2 = (f32[4,3,8,512]{3,2,1,0:T(8,128)S(1)}, f32[4,3,8,512]{3,2,1,0:T(8,128)}, u32[]{:S(2)}) copy-start(f32[4,3,8,512]{3,2,1,0:T(8,128)} %get-tuple-element.11) | copy-start | bytes 589828

commit v2 on v1

--- a/solution.py
+++ b/solution.py
@@ -2,6 +2,7 @@
 
 import jax
 import jax.numpy as jnp
+import numpy as np
 from jax import lax
 from jax.experimental import pallas as pl
 from jax.experimental.pallas import tpu as pltpu
@@ -130,18 +131,12 @@
     per_head,
     x_ref,
     gain_ref,
-    perm_ref,
     spread_ref,
-    bias_ref,
-    decay_ref,
-    skip_ref,
-    norm_ref,
-    conv_x_ref,
-    conv_bc_ref,
-    hist_x_in,
-    hist_bc_in,
+    pack_ref,
+    pack_bc_ref,
     w_inner_hbm,
-    w_aux_hbm,
+    w_state_hbm,
+    w_step_hbm,
     w_out_hbm,
     state_hbm,
     out_ref,
@@ -149,11 +144,11 @@
     hist_x,
     hist_all,
     w_in,
-    w_aux,
+    w_st,
+    w_dt,
     w_o,
     current,
     gathered,
-    acc,
     parts,
     part_in,
     norm_out,
@@ -170,32 +165,42 @@
     mi = lax.axis_index("mp")
     hi = lax.axis_index("heads")
     rows, feat = x_ref.shape
-    chan = norm_ref.shape[1]
     part = w_o.shape[2]
-    block = perm_ref.shape[0]
-    n_blocks = w_in.shape[2] // block
-    n_state = w_aux.shape[2] - LANES
+    chan = n_local * part
+    n_state = w_st.shape[1]
     state_size = n_state // 2
 
+    w_dt[...] = jnp.zeros_like(w_dt)
     loads_in = []
     for d in range(n_heads):
         owner = lax.rem(hi - d + n_heads, n_heads)
         span = pl.ds(pl.multiple_of(owner * feat, feat), feat)
-        a = pltpu.make_async_copy(w_inner_hbm.at[span], w_in.at[d], load_sem.at[0, d])
-        b = pltpu.make_async_copy(w_aux_hbm.at[span], w_aux.at[d], load_sem.at[1, d])
-        a.start()
-        loads_in.append((a, b))
-    for a, b in loads_in:
-        b.start()
-    loads_rest = [pltpu.make_async_copy(state_hbm, hidden, load_sem.at[2, 0])]
+        copies = [
+            pltpu.make_async_copy(
+                w_inner_hbm.at[:, :, m * part : (m + 1) * part, span],
+                w_in.at[d, m],
+                load_sem.at[4 + m, d],
+            )
+            for m in range(n_mp)
+        ]
+        copies.append(pltpu.make_async_copy(w_state_hbm.at[:, span], w_st.at[d], load_sem.at[0, d]))
+        copies.append(
+            pltpu.make_async_copy(
+                w_step_hbm.at[:, span], w_dt.at[d, 0:n_local], load_sem.at[1, d]
+            )
+        )
+        for c in copies:
+            c.start()
+        loads_in.append(copies)
+    load_state = pltpu.make_async_copy(state_hbm, hidden, load_sem.at[2, 0])
+    load_state.start()
+    loads_out = []
     for d in range(n_mp):
         owner = lax.rem(mi - d + n_mp, n_mp)
         span = pl.ds(pl.multiple_of(owner * part, part), part)
-        loads_rest.append(
-            pltpu.make_async_copy(w_out_hbm.at[:, span], w_o.at[d], load_sem.at[3, d])
-        )
-    for c in loads_rest:
+        c = pltpu.make_async_copy(w_out_hbm.at[:, span], w_o.at[d], load_sem.at[3, d])
         c.start()
+        loads_out.append(c)
 
     barrier = pltpu.get_barrier_semaphore()
     for d in range(1, n_heads):
@@ -212,28 +217,9 @@
     pl.semaphore_wait(barrier, n_heads + n_mp - 2)
 
     current[...] = x_ref[...]
-    hist_x[...] = hist_x_in[...]
-    hist_bc[...] = hist_bc_in[...]
-
-    row_chunk = min(feat, 256)
-    for d in range(n_heads):
-        loads_in[d][0].wait()
-
-        @pl.loop(0, n_blocks)
-        def _(b):
-            cols = pl.ds(pl.multiple_of(b * block, block), block)
-            for r in range(0, feat, row_chunk):
-                moved = jnp.dot(
-                    w_in[d, r : r + row_chunk, cols],
-                    perm_ref[...],
-                    preferred_element_type=jnp.float32,
-                )
-                w_in[d, r : r + row_chunk, cols] = moved.astype(jnp.bfloat16)
-
-    for a, b in loads_in:
-        b.wait()
-    for c in loads_rest:
-        c.wait()
+    for k in range(3):
+        hist_x[k] = pack_ref[8 + k * rows : 8 + (k + 1) * rows]
+        hist_bc[k] = pack_bc_ref[8 + k * rows : 8 + (k + 1) * rows]
 
     def exchange(phase, axis, me, n, source, dest):
         copies = []
@@ -251,19 +237,29 @@
             copies.append(c)
         return copies
 
-    chunk = block
+    def in_dot(x, w):
+        return lax.dot_general(
+            x, w, (((1,), (1,)), ((), ())), preferred_element_type=jnp.float32
+        )
+
+    def in_weight(d, m):
+        return w_in[d, m].reshape(2 * chan, feat)
 
     def step(s, carry):
         cur = current[...]
         sent = exchange(0, "heads", hi, n_heads, lambda t: current, gathered)
         first = (cur * gain_ref[hi]).astype(jnp.bfloat16)
         sq = jnp.sum(cur * cur, axis=1, keepdims=True)
-        for b in range(n_blocks):
-            lo = b * chunk
-            acc[:, lo : lo + chunk] = jnp.dot(
-                first, w_in[0, :, lo : lo + chunk], preferred_element_type=jnp.float32
-            )
-        aux = jnp.dot(first, w_aux[0], preferred_element_type=jnp.float32)
+
+        @pl.when(s == 0)
+        def _():
+            for c in loads_in[0]:
+                c.wait()
+
+        for m in range(n_mp):
+            parts[m, :, : 2 * chan] = in_dot(first, in_weight(0, m))
+        aux = in_dot(first, w_st[0])
+        tail = in_dot(first, w_dt[0])
         later = []
         for d in range(1, n_heads):
             sent[d - 1].wait()
@@ -271,23 +267,25 @@
             owner = lax.rem(hi - d + n_heads, n_heads)
             later.append((v * gain_ref[owner]).astype(jnp.bfloat16))
             sq = sq + jnp.sum(v * v, axis=1, keepdims=True)
-        for b in range(n_blocks):
-            lo = b * chunk
-            total = acc[:, lo : lo + chunk]
+
+        @pl.when(s == 0)
+        def _():
+            for copies in loads_in[1:]:
+                for c in copies:
+                    c.wait()
+
+        for m in range(n_mp):
+            total = parts[m, :, : 2 * chan]
             for d in range(1, n_heads):
-                total = total + jnp.dot(
-                    later[d - 1],
-                    w_in[d, :, lo : lo + chunk],
-                    preferred_element_type=jnp.float32,
-                )
-            for m in range(n_mp):
-                parts[m, :, b * LANES : (b + 1) * LANES] = total[:, m * LANES : (m + 1) * LANES]
+                total = total + in_dot(later[d - 1], in_weight(d, m))
+            parts[m, :, : 2 * chan] = total
         for d in range(1, n_heads):
-            aux = aux + jnp.dot(later[d - 1], w_aux[d], preferred_element_type=jnp.float32)
+            aux = aux + in_dot(later[d - 1], w_st[d])
+            tail = tail + in_dot(later[d - 1], w_dt[d])
         lane = lax.broadcasted_iota(jnp.int32, (rows, LANES), 1)
-        tail = jnp.where(lane == n_local, sq, aux[:, n_state:])
+        tail = jnp.where(lane == n_local, sq, tail)
         for m in range(n_mp):
-            parts[m, :, 2 * chan : 2 * chan + n_state] = aux[:, :n_state]
+            parts[m, :, 2 * chan : 2 * chan + n_state] = aux
             parts[m, :, 2 * chan + n_state :] = tail
 
         sent = exchange(1, "mp", mi, n_mp, lambda t: parts.at[t], part_in)
@@ -310,24 +308,29 @@
             hist[0] = old[1]
             hist[1] = old[2]
             hist[2] = new
-            v = old[0] * kernel[0] + old[1] * kernel[1] + old[2] * kernel[2] + new * kernel[3]
+            v = old[0] * kernel[0:1] + old[1] * kernel[1:2] + old[2] * kernel[2:3] + new * kernel[3:4]
             return silu(v)
 
-        conv_x = conv(hist_x, new_x, conv_x_ref)
-        conv_bc = conv(hist_bc, new_bc, conv_bc_ref)
+        conv_x = conv(hist_x, new_x, pack_ref)
+        conv_bc = conv(hist_bc, new_bc, pack_bc_ref)
         spread = jnp.dot(
             tail,
             spread_ref[...],
             preferred_element_type=jnp.float32,
             precision=lax.Precision.HIGHEST,
         )
-        raw = spread * inv + bias_ref[...]
+        raw = spread * inv + pack_ref[5:6]
         dt = jnp.maximum(raw, 0.0) + jnp.log1p(jnp.exp(-jnp.abs(raw)))
-        decay = jnp.exp(-dt * decay_ref[...])
+        decay = jnp.exp(-dt * pack_ref[6:7])
         driven = dt * conv_x
         b_cols = jnp.transpose(conv_bc[:, :state_size])
         c_cols = jnp.transpose(conv_bc[:, state_size:])
         part_n = min(state_size, 64)
+
+        @pl.when(s == 0)
+        def _():
+            load_state.wait()
+
         for r in range(rows):
             sums = [jnp.zeros((part_n, LANES), jnp.float32) for _ in range(chan // LANES)]
             for n0 in range(0, state_size, part_n):
@@ -345,10 +348,10 @@
                 reading_s[r : r + 1, c * LANES : (c + 1) * LANES] = jnp.sum(
                     sums[c], axis=0, keepdims=True
                 )
-        reading = reading_s[...] + skip_ref[...] * conv_x
+        reading = reading_s[...] + pack_ref[7:8] * conv_x
         gated = reading * silu(gate)
         group_sq = jnp.sum(gated * gated, axis=1, keepdims=True)
-        mine = (gated * norm_ref[...]).astype(jnp.bfloat16)
+        mine = (gated * pack_ref[4:5]).astype(jnp.bfloat16)
         norm_out[:, :chan] = mine.astype(jnp.float32)
         norm_out[:, chan:] = jnp.broadcast_to(group_sq, (rows, LANES))
 
@@ -357,6 +360,11 @@
         def out_weight(d, b):
             w = w_o[d, :, :, b * feat : (b + 1) * feat]
             return w.reshape(w.shape[0] * w.shape[1], feat)
+
+        @pl.when(s == 0)
+        def _():
+            for c in loads_out:
+                c.wait()
 
         for b in range(n_heads):
             out_parts[b] = jnp.dot(mine, out_weight(0, b), preferred_element_type=jnp.float32)
@@ -421,18 +429,25 @@
     chan = n_local * part
     n_state = 2 * state_size
     hi = lax.axis_index("heads")
-    in_block = LANES // part
-    block = in_block * per_head
-    i_in = jnp.arange(block)
-    head, slot, lane = i_in // per_head, (i_in % per_head) // part, i_in % part
-    place = slot * LANES + head * part + lane
-    perm = (place[:, None] == jnp.arange(block)[None, :]).astype(bf16)
-    spread = (jnp.arange(LANES)[:, None] == (jnp.arange(chan) // part)[None, :]).astype(f32)
+    spread = (np.arange(LANES)[:, None] == (np.arange(chan) // part)[None, :]).astype(np.float32)
     own_state = lax.dynamic_slice_in_dim(w_state, hi, 1, 2).reshape(width, n_state)
-    aux = jnp.concatenate([own_state, jnp.pad(w_step, ((0, 0), (0, LANES - n_local)))], axis=1)
-    wide = lambda v: jnp.repeat(v, part)[None]
-    own_conv = lax.dynamic_slice_in_dim(conv_state_weight, hi, 1, 2).reshape(4, 1, n_state)
-    own_hist = lax.dynamic_slice_in_dim(history_state, hi, 1, 3).reshape(rows, 3, n_state)
+    heads_wide = jnp.stack([step_bias, decay_scale, skip_gain])
+    pack = jnp.concatenate(
+        [
+            conv_inner,
+            norm_gain[None],
+            jnp.broadcast_to(heads_wide[:, :, None], (3, n_local, part)),
+            jnp.swapaxes(history_inner, 0, 1).reshape(3 * rows, n_local, part).astype(f32),
+        ]
+    ).reshape(8 + 3 * rows, chan)
+    own_conv = lax.dynamic_slice_in_dim(conv_state_weight, hi, 1, 2)[:, :, 0]
+    own_hist = lax.dynamic_slice_in_dim(history_state, hi, 1, 3)[:, :, :, 0].astype(f32)
+    pack_bc = jnp.concatenate(
+        [
+            jnp.pad(own_conv, ((0, 4), (0, 0), (0, 0))),
+            jnp.swapaxes(own_hist, 0, 1).reshape(3 * rows, 2, state_size),
+        ]
+    ).reshape(8 + 3 * rows, n_state)
     vmem = pl.BlockSpec(memory_space=pltpu.VMEM)
     hbm = pl.BlockSpec(memory_space=pl.ANY)
     shape = jax.ShapeDtypeStruct
@@ -444,15 +459,15 @@
             shape((3, rows, chan), f32),
             shape((n_heads, 3, rows, n_state), f32),
         ),
-        in_specs=[vmem] * 12 + [hbm] * 4,
+        in_specs=[vmem] * 5 + [hbm] * 5,
         out_specs=(vmem,) * 4,
         scratch_shapes=[
-            pltpu.VMEM((n_heads, feat, 2 * n_local * per_head), bf16),
-            pltpu.VMEM((n_heads, feat, n_state + LANES), bf16),
+            pltpu.VMEM((n_heads, n_mp, 2, n_local, part, feat), bf16),
+            pltpu.VMEM((n_heads, n_state, feat), bf16),
+            pltpu.VMEM((n_heads, LANES, feat), bf16),
             pltpu.VMEM((n_mp, n_local, part, w_out.shape[2]), bf16),
             pltpu.VMEM((rows, feat), f32),
             pltpu.VMEM((n_heads, rows, feat), f32),
-            pltpu.VMEM((rows, 2 * n_local * per_head), f32),
             pltpu.VMEM((n_mp, rows, 2 * chan + n_state + LANES), f32),
             pltpu.VMEM((n_mp, rows, 2 * chan + n_state + LANES), f32),
             pltpu.VMEM((rows, chan + LANES), f32),
@@ -462,7 +477,7 @@
             pltpu.VMEM((3, rows, n_state), f32),
             pltpu.VMEM((n_heads, 3, rows, n_state), f32),
             pltpu.VMEM((rows, chan), f32),
-            pltpu.SemaphoreType.DMA((4, max(n_mp, n_heads))),
+            pltpu.SemaphoreType.DMA((4 + n_mp, max(n_mp, n_heads))),
             pltpu.SemaphoreType.DMA((5, max(n_mp, n_heads))),
             pltpu.SemaphoreType.DMA((5, max(n_mp, n_heads))),
         ],
@@ -472,18 +487,12 @@
     )(
         stream.astype(f32),
         in_gain.reshape(n_heads, 1, feat),
-        perm,
         spread,
-        wide(step_bias),
-        wide(decay_scale),
-        wide(skip_gain),
-        norm_gain.reshape(1, chan),
-        conv_inner.reshape(4, 1, chan),
-        own_conv,
-        jnp.swapaxes(history_inner.reshape(rows, 3, chan), 0, 1).astype(f32),
-        jnp.swapaxes(own_hist, 0, 1).astype(f32),
-        w_inner.reshape(width, 2 * n_local * per_head),
-        aux,
+        pack,
+        pack_bc,
+        jnp.transpose(w_inner, (1, 2, 3, 0)),
+        jnp.transpose(own_state),
+        jnp.transpose(w_step),
         w_out,
         jnp.swapaxes(ssm_state.reshape(rows, chan, state_size), 1, 2),
     )
@@ -505,6 +514,9 @@
             n_local == NH // NG
             and n_heads == w_state.shape[2]
             and n_local < LANES
+            and n_local % 16 == 0
+            and part % 16 == 0
+            and stream.shape[0] % 8 == 0
             and LANES % part == 0
             and per_head == part * n_mp
             and (n_local * part) % LANES == 0

time: 263 us -> 232 us (0.88)
  local copies, waits for them, and re-layouts: 64.1 us -> 33.4 us
  Pallas kernels: 188 us -> 192 us
  other arithmetic: 8.58 us -> 5.19 us
    reshape x4 -> x0, local copies, waits for them, and re-layouts: 25.3 us -> none  [the longest x1 21.4 us: fused_body(): w_inner.reshape(width, 2 * n_local * per_head)]
    dynamic_slice x1 -> x2, local copies, waits for them, and re-layouts: 7.26 us -> 17.8 us  [fused_body(): lax.dynamic_slice_in_dim(w_state, hi, 1, 2).reshape(width, n_state)]
    unnamed x14 -> x12, local copies, waits for them, and re-layouts: 12.6 us -> 2.4 us
    pallas_call x1, Pallas kernels: 188 us -> 192 us  [fused_body(): pl.pallas_call(functools.partial(fused_kernel, n_mp, n_heads, n_local, pe...]
    concatenate x1 -> x2, other arithmetic: 3.37 us -> 0.67 us  [the longest x1 0.67 us: fused_body(): jnp.concatenate([conv_inner, norm_gain[None], jnp.broadcast_to(heads_wide...]
where the time goes in v2:
time: 232 us; the launch traced here: 231 us
  Pallas kernels  192 us (83%)
  local copies, waits for them, and re-layouts  33.4 us (14%)
  other arithmetic  5.19 us (2%)
    pallas_call x1, Pallas kernels, fused_body(): pl.pallas_call(functools.partial(fused_kernel, n_mp, n_heads, n_local, pe...  192 us
    dynamic_slice x2, local copies, waits for them, and re-layouts, fused_body(): lax.dynamic_slice_in_dim(w_state, hi, 1, 2).reshape(width, n_state)  17.8 us
    transpose x1, local copies, waits for them, and re-layouts, fused_body(): jnp.swapaxes(hidden, 1, 2).reshape(ssm_state.shape)  5.39 us
    reshape x1, local copies, waits for them, and re-layouts, fused_body(): ssm_state.reshape(rows, chan, state_size)  5.34 us

profile of v2, /device:TPU:0, one launch (start us, length us, event | category | flops | bytes accessed | tf_op | source)
XLA Modules:
  0.0 231.3 jit_solution(7007020514900383164)
XLA Ops:
  0.6 0.0 copy-start
  0.7 0.7 pad_maximum_fusion.2
  1.4 0.8 constant_dynamic-slice_fusion.2
  2.2 1.3 convert_element_type.40.x_ref
  3.5 0.8 copy.30
  4.3 0.1 concatenate.21
  4.3 0.1 broadcast_in_dim.2
  4.4 0.1 concatenate.22
  4.5 0.1 constant_dynamic-slice_fusion.1
  4.6 0.8 copy.29
  5.4 0.1 concatenate.20
  5.5 0.9 convert_bitcast_fusion
  6.5 0.2 copy.31
  6.6 0.2 reshape.47
  6.9 0.7 pad_maximum_fusion
  7.5 7.2 %constant_dynamic-slice_fusion = bf16[2048,2,1,256]{3,2,1,0:T(2,128)(2,1)} fusion(bf16[2048,2,4,256]{3,2,1,0:T(4,128)(2,1)} %param.19, s32[]{:T(128)S(6)} %select_n.2), kind=kLoop, calls=%fused_computation.10 | loop fusion | bytes 4194308 | tf_op jit(solution)/shard_map/dynamic_slice | solution.py:433
  14.8 10.6 %copy.33 = bf16[2048,2,1,256]{0,3,1,2:T(8,128)(2,1)} copy(bf16[2048,2,1,256]{3,2,1,0:T(2,128)(2,1)} %constant_dynamic-slice_fusion) | data formatting | bytes 4194304 | tf_op jit(solution)/shard_map/dynamic_slice | solution.py:433
  25.3 5.3 %copy.34 = f32[8,512,256]{1,2,0:T(8,128)} copy(f32[8,512,256]{2,1,0:T(8,128)} %bitcast.42) | data formatting | bytes 8388608 | tf_op jit(solution)/shard_map/reshape | solution.py:497
  30.7 192.0 %shard_map.183 = (f32[8,8,512]{2,1,0:T(8,128)}, f32[8,256,512]{2,1,0:T(8,128)}, f32[3,8,512]{2,1,0:T(8,128)}, f32[4,3,8,512]{3,2,1,0:T(8,128)}) custom-call(f32[8,512]{1,0:T(8,128)} %convert_element_type.40.x_ref, f32[4,1,512]{2,1,0:T(1,128)} %bitcast.51, f32[128,512]{1,0:T(8,128)} %constant.12.clone.spread_ref, f32[32,512]{1,0:T(8,128)} %get-tuple-element.20.pack_ref, ...), custom_call_target="tpu_custom_call" | custom-call | tf_op jit(solution)/shard_map/pallas_call | solution.py:454
  222.7 1.5 convert_element_type.45
  224.2 5.4 %copy.35 = f32[8,512,256]{2,1,0:T(8,128)} copy(f32[8,512,256]{1,2,0:T(8,128)} %bitcast.44) | data formatting | bytes 8388608 | tf_op jit(solution)/shard_map/transpose | solution.py:502
  229.6 0.7 copy.46
  230.3 0.2 convert_element_type.48
  230.5 0.8 copy.37
  (11 shorter events, 0.0 us)
Async XLA Ops:
  0.6 3.9 %copy-start = (bf16[8,3,2,4,256]{4,3,2,1,0:T(4,128)(2,1)S(1)}, bf16[8,3,2,4,256]{4,3,2,1,0:T(4,128)(2,1)}, u32[]{:S(2)}) copy-start(bf16[8,3,2,4,256]{4,3,2,1,0:T(4,128)(2,1)} %param.27) | copy-start | bytes 294916
  224.2 5.4 %copy-start.2 = (f32[3,8,512]{2,1,0:T(8,128)S(1)}, f32[3,8,512]{2,1,0:T(8,128)}, u32[]{:S(2)}) copy-start(f32[3,8,512]{2,1,0:T(8,128)} %get-tuple-element.10) | copy-start | bytes 147460
  224.2 5.4 %copy-start.1 = (f32[4,3,8,512]{3,2,1,0:T(8,128)S(1)}, f32[4,3,8,512]{3,2,1,0:T(8,128)}, u32[]{:S(2)}) copy-start(f32[4,3,8,512]{3,2,1,0:T(8,128)} %get-tuple-element.11) | copy-start | bytes 589828

commit v3 on v2

--- a/solution.py
+++ b/solution.py
@@ -167,7 +167,7 @@
     rows, feat = x_ref.shape
     part = w_o.shape[2]
     chan = n_local * part
-    n_state = w_st.shape[1]
+    n_state = w_st.shape[2]
     state_size = n_state // 2
 
     w_dt[...] = jnp.zeros_like(w_dt)
@@ -183,7 +183,7 @@
             )
             for m in range(n_mp)
         ]
-        copies.append(pltpu.make_async_copy(w_state_hbm.at[:, span], w_st.at[d], load_sem.at[0, d]))
+        copies.append(pltpu.make_async_copy(w_state_hbm.at[span], w_st.at[d], load_sem.at[0, d]))
         copies.append(
             pltpu.make_async_copy(
                 w_step_hbm.at[:, span], w_dt.at[d, 0:n_local], load_sem.at[1, d]
@@ -258,7 +258,7 @@
 
         for m in range(n_mp):
             parts[m, :, : 2 * chan] = in_dot(first, in_weight(0, m))
-        aux = in_dot(first, w_st[0])
+        aux = jnp.dot(first, w_st[0], preferred_element_type=jnp.float32)
         tail = in_dot(first, w_dt[0])
         later = []
         for d in range(1, n_heads):
@@ -280,7 +280,7 @@
                 total = total + in_dot(later[d - 1], in_weight(d, m))
             parts[m, :, : 2 * chan] = total
         for d in range(1, n_heads):
-            aux = aux + in_dot(later[d - 1], w_st[d])
+            aux = aux + jnp.dot(later[d - 1], w_st[d], preferred_element_type=jnp.float32)
             tail = tail + in_dot(later[d - 1], w_dt[d])
         lane = lax.broadcasted_iota(jnp.int32, (rows, LANES), 1)
         tail = jnp.where(lane == n_local, sq, tail)
@@ -430,7 +430,14 @@
     n_state = 2 * state_size
     hi = lax.axis_index("heads")
     spread = (np.arange(LANES)[:, None] == (np.arange(chan) // part)[None, :]).astype(np.float32)
-    own_state = lax.dynamic_slice_in_dim(w_state, hi, 1, 2).reshape(width, n_state)
+    chosen = (jnp.arange(n_groups) == hi)[None, :, None]
+    own_state = jnp.concatenate(
+        [
+            jnp.sum(jnp.where(chosen, w_state[:, k].astype(f32), 0.0), axis=1).astype(bf16)
+            for k in range(2)
+        ],
+        axis=1,
+    )
     heads_wide = jnp.stack([step_bias, decay_scale, skip_gain])
     pack = jnp.concatenate(
         [
@@ -463,7 +470,7 @@
         out_specs=(vmem,) * 4,
         scratch_shapes=[
             pltpu.VMEM((n_heads, n_mp, 2, n_local, part, feat), bf16),
-            pltpu.VMEM((n_heads, n_state, feat), bf16),
+            pltpu.VMEM((n_heads, feat, n_state), bf16),
             pltpu.VMEM((n_heads, LANES, feat), bf16),
             pltpu.VMEM((n_mp, n_local, part, w_out.shape[2]), bf16),
             pltpu.VMEM((rows, feat), f32),
@@ -491,7 +498,7 @@
         pack,
         pack_bc,
         jnp.transpose(w_inner, (1, 2, 3, 0)),
-        jnp.transpose(own_state),
+        own_state,
         jnp.transpose(w_step),
         w_out,
         jnp.swapaxes(ssm_state.reshape(rows, chan, state_size), 1, 2),

time: 232 us -> 232 us (level)
  other arithmetic: 5.19 us -> 25 us
  local copies, waits for them, and re-layouts: 33.4 us -> 15.6 us
    reduce_sum x0 -> x1, other arithmetic: none -> 18.4 us  [fused_body(): jnp.sum(jnp.where(chosen, w_state[:, k].astype(f32), 0.0), axis=1)]
    dynamic_slice x2 -> x0, local copies, waits for them, and re-layouts: 17.8 us -> none  [fused_body(): lax.dynamic_slice_in_dim(w_state, hi, 1, 2).reshape(width, n_state)]
where the time goes in v3:
time: 232 us; the launch traced here: 231 us
  Pallas kernels  190 us (82%)
  other arithmetic  25 us (11%)
  local copies, waits for them, and re-layouts  15.6 us (7%)
    pallas_call x1, Pallas kernels, fused_body(): pl.pallas_call(functools.partial(fused_kernel, n_mp, n_heads, n_local, pe...  190 us
    reduce_sum x1, other arithmetic, fused_body(): jnp.sum(jnp.where(chosen, w_state[:, k].astype(f32), 0.0), axis=1)  18.4 us
    transpose x1, local copies, waits for them, and re-layouts, fused_body(): jnp.swapaxes(hidden, 1, 2).reshape(ssm_state.shape)  5.39 us
    reshape x1, local copies, waits for them, and re-layouts, fused_body(): ssm_state.reshape(rows, chan, state_size)  5.34 us

profile of v3, /device:TPU:0, one launch (start us, length us, event | category | flops | bytes accessed | tf_op | source)
XLA Modules:
  0.0 231.2 jit_solution(840572094730258016)
XLA Ops:
  0.6 0.0 copy-start
  0.7 0.7 pad_maximum_fusion.3
  1.4 0.8 constant_dynamic-slice_fusion.1
  2.2 1.3 convert_element_type.58.x_ref
  3.5 0.8 copy.30
  4.3 0.1 concatenate.24
  4.4 0.1 broadcast_in_dim.24
  4.4 0.1 concatenate.25
  4.5 0.1 constant_dynamic-slice_fusion
  4.6 0.8 copy.29
  5.5 0.1 concatenate.23
  5.6 0.9 convert_bitcast_fusion
  6.5 0.2 copy.31
  6.7 0.2 reshape.51
  6.9 0.7 pad_maximum_fusion.1
  7.5 18.4 %fusion.1 = (bf16[2048,256]{1,0:T(8,128)(2,1)S(1)}, bf16[2048,256]{1,0:T(8,128)(2,1)S(1)}) fusion(bf16[2048,2,4,256]{3,2,1,0:T(4,128)(2,1)} %param.19, pred[4]{0:T(512)(128)(4,1)S(1)} %iota_compare_fusion), kind=kLoop, calls=%fused_computation.3 | loop fusion | flops 11534336 | bytes 10485764 | tf_op jit(solution)/shard_map/reduce_sum | solution.py:436
  25.9 1.5 pad_maximum_fusion.w_state_hbm
  27.4 5.3 %copy.34 = f32[8,512,256]{1,2,0:T(8,128)} copy(f32[8,512,256]{2,1,0:T(8,128)} %bitcast.46) | data formatting | bytes 8388608 | tf_op jit(solution)/shard_map/reshape | solution.py:504
  32.7 189.9 %shard_map.183 = (f32[8,8,512]{2,1,0:T(8,128)}, f32[8,256,512]{2,1,0:T(8,128)}, f32[3,8,512]{2,1,0:T(8,128)}, f32[4,3,8,512]{3,2,1,0:T(8,128)}) custom-call(f32[8,512]{1,0:T(8,128)} %convert_element_type.58.x_ref, f32[4,1,512]{2,1,0:T(1,128)} %bitcast.55, f32[128,512]{1,0:T(8,128)} %constant.13.clone.spread_ref, f32[32,512]{1,0:T(8,128)} %get-tuple-element.22.pack_ref, ...), custom_call_target="tpu_custom_call" | custom-call | tf_op jit(solution)/shard_map/pallas_call | solution.py:461
  222.6 1.5 convert_element_type.69
  224.2 5.4 %copy.35 = f32[8,512,256]{2,1,0:T(8,128)} copy(f32[8,512,256]{1,2,0:T(8,128)} %bitcast.48) | data formatting | bytes 8388608 | tf_op jit(solution)/shard_map/transpose | solution.py:509
  229.6 0.7 copy.47
  230.3 0.2 convert_element_type.72
  230.5 0.8 copy.37
  (12 shorter events, 0.1 us)
Async XLA Ops:
  0.6 3.9 %copy-start = (bf16[8,3,2,4,256]{4,3,2,1,0:T(4,128)(2,1)S(1)}, bf16[8,3,2,4,256]{4,3,2,1,0:T(4,128)(2,1)}, u32[]{:S(2)}) copy-start(bf16[8,3,2,4,256]{4,3,2,1,0:T(4,128)(2,1)} %param.27) | copy-start | bytes 294916
  224.2 5.4 %copy-start.2 = (f32[3,8,512]{2,1,0:T(8,128)S(1)}, f32[3,8,512]{2,1,0:T(8,128)}, u32[]{:S(2)}) copy-start(f32[3,8,512]{2,1,0:T(8,128)} %get-tuple-element.10) | copy-start | bytes 147460
  224.2 5.4 %copy-start.1 = (f32[4,3,8,512]{3,2,1,0:T(8,128)S(1)}, f32[4,3,8,512]{3,2,1,0:T(8,128)}, u32[]{:S(2)}) copy-start(f32[4,3,8,512]{3,2,1,0:T(8,128)} %get-tuple-element.11) | copy-start | bytes 589828
